TPU v7x, 32 devices: a whole 2x2x4 slice. The times are simulated.
32 devices in a mesh: dp: 4 (over z), proto: 8 (over y, x, core).
Axes of the slice: x: 2, y: 2, z: 4, core: 2. Of those that a mesh axis runs over, the one named last changes fastest.
Arguments:
- embeddings: bfloat16 [8192, 2560], P('proto', 'dp'), may hold values from -26 to 26
- table: bfloat16 [32768, 2560], P('proto', 'dp'), may hold values from -5 to 5
- tile_lists: int32 [8, 8], replicated, may hold values from 0 to 255, as said below
- labels: int32 [8192], P('proto'), may hold values from 0 to 32767, as said below
Outputs:
- loss: float32 [], replicated
- grad_emb: bfloat16 [8192, 2560], P('proto', 'dp')
- grad_table: bfloat16 [32768, 2560], P('proto', 'dp')
Inputs may be any that keep to these rules, and one draw needn't show every extreme that they name: `tile_lists`: each block's 8 tile ids are distinct and fall on exactly 4 owners (owner = id // 32), each of those owners holding exactly 2 of them. `labels`: the tile of each row's label (label // 128) is in the list of the row's block.
All inputs are finite; a program needn't handle non-finite values.
Results may differ from a plain program's by a relative error of at most 0.0025.
The roundings to bfloat16 on the way count: a program that leaves them out, or rounds other values in their place, can miss the bound.
Values may be sent and summed in bfloat16 or wider, within the bound.
A program may use at most 128 MiB of HBM per device.

v0:
```python
import math
import jax
import jax.numpy as jnp
from jax import lax
from jax.sharding import PartitionSpec as P

D = 2560
TILE = 128
CAP = 2


def slot_plan(ids, tiles_here):
    owners = ids // tiles_here
    local = ids % tiles_here
    count = ids.shape[-1]
    before = jnp.arange(count)[:, None] > jnp.arange(count)[None, :]
    earlier = (owners[..., :, None] == owners[..., None, :]) & before
    rank = jnp.sum(earlier.astype(jnp.int32), axis=-1)
    return (owners, local, rank)


def softmax_terms(scores, ids, lab, list_len):
    hit = (ids[None, :] == (lab // TILE)[:, None]).astype(jnp.int32)
    column = (
        jnp.sum(hit * (jnp.arange(list_len, dtype=jnp.int32) * TILE)[None, :], axis=1) + lab % TILE
    )
    onehot = (jnp.arange(list_len * TILE, dtype=jnp.int32)[None, :] == column[:, None]).astype(
        jnp.float32
    )
    top = jnp.max(scores, axis=1, keepdims=True)
    expo = jnp.exp(scores - top)
    total = jnp.sum(expo, axis=1, keepdims=True)
    lse = top[:, 0] + jnp.log(total[:, 0])
    target = jnp.sum(scores * onehot, axis=1)
    dz_rows = (expo / total - onehot).astype(jnp.bfloat16)
    return (jnp.sum(lse - target), dz_rows)


def body(embeddings, table, tile_lists, labels):
    block_rows, width = embeddings.shape
    list_len = tile_lists.shape[1]
    tiles_here = table.shape[0] // TILE
    groups = lax.axis_size("proto")
    dp_count = lax.axis_size("dp")
    rows_dev = block_rows // dp_count
    total_rows = block_rows * groups
    me = lax.axis_index("proto")
    part = lax.axis_index("dp")
    inv_scale = 1.0 / math.sqrt(D)
    owners, local, rank = slot_plan(tile_lists, tiles_here)
    match = (owners == me)[:, :, None] & (
        rank[:, :, None] == jnp.arange(CAP, dtype=jnp.int32)[None, None, :]
    )
    select = jnp.sum(match.astype(jnp.int32) * local[:, :, None], axis=1)
    shaped_table = table.reshape(tiles_here, TILE, width)
    outgoing = jnp.take(shaped_table, select.reshape(-1), axis=0).reshape(groups, CAP, TILE, width)
    incoming = lax.all_to_all(outgoing, "proto", split_axis=0, concat_axis=0, tiled=True)
    my_ids = lax.dynamic_index_in_dim(tile_lists, me, 0, keepdims=False)
    my_owner = lax.dynamic_index_in_dim(owners, me, 0, keepdims=False)
    my_rank = lax.dynamic_index_in_dim(rank, me, 0, keepdims=False)
    flat_slot = my_owner * CAP + my_rank
    tiles = jnp.take(incoming.reshape(groups * CAP, TILE, width), flat_slot, axis=0).reshape(
        list_len * TILE, width
    )
    scores = (
        lax.psum_scatter(
            lax.dot_general(
                embeddings, tiles, (((1,), (1,)), ((), ())), preferred_element_type=jnp.float32
            ),
            "dp",
            scatter_dimension=0,
            tiled=True,
        )
        * inv_scale
    )
    my_labels = lax.dynamic_slice_in_dim(labels, part * rows_dev, rows_dev, 0)
    loss_part, dz_rows = softmax_terms(scores, my_ids, my_labels, list_len)
    dz_block = lax.all_gather(dz_rows, "dp", axis=0, tiled=True)
    loss = lax.psum(loss_part, ("dp", "proto")) / total_rows
    grad_emb = jnp.dot(dz_block, tiles, preferred_element_type=jnp.float32).astype(jnp.bfloat16)
    piece = lax.dot_general(
        dz_block, embeddings, (((0,), (0,)), ((), ())), preferred_element_type=jnp.float32
    ).astype(jnp.bfloat16)
    returning = (
        jnp.zeros((groups * CAP, TILE, width), jnp.bfloat16)
        .at[flat_slot]
        .set(piece.reshape(list_len, TILE, width))
    )
    returned = lax.all_to_all(
        returning.reshape(groups, CAP, TILE, width),
        "proto",
        split_axis=0,
        concat_axis=0,
        tiled=True,
    )
    accum = (
        jnp.zeros((tiles_here, TILE, width), jnp.float32)
        .at[select.reshape(-1)]
        .add(returned.reshape(groups * CAP, TILE, width))
    )
    grad_table = accum.reshape(tiles_here * TILE, width).astype(jnp.bfloat16)
    return (loss, grad_emb, grad_table)


def solution(mesh):
    placed = (P("proto", "dp"), P("proto", "dp"), P(), P("proto"))
    return jax.shard_map(
        body,
        mesh=mesh,
        in_specs=placed,
        out_specs=(P(), P("proto", "dp"), P("proto", "dp")),
        check_vma=False,
    )
```

profile of v0, /device:TPU:0, one launch (start us, length us, event | category | flops | bytes accessed | tf_op | source)
XLA Modules:
  0.0 308.0 jit_solution(9859530231807013274)
XLA Ops:
  7.2 0.0 copy-start
  7.2 0.8 add_select_fusion
  8.0 0.7 broadcast_compare_fusion
  8.7 0.3 convert_reduce_fusion
  9.0 0.2 select_reduce_fusion.2
  9.1 0.1 copy.8
  9.2 0.1 copy.7
  9.3 0.1 reshape.136
  9.4 4.8 %gather_fusion = bf16[16,128,640]{2,1,0:T(8,128)(2,1)} fusion(bf16[32,128,640]{2,1,0:T(8,128)(2,1)} %bitcast.36, s32[1024]{0:T(1024)S(1)} %pad_clamp_fusion.1), kind=kCustom, calls=%fused_computation | custom fusion | bytes 5242944 | tf_op jit(solution)/shard_map/jit(_take)/gather | solution.py:56
  14.3 3.6 %broadcast_select_fusion = bf16[8,2,128,640]{3,2,1,0:T(8,128)(2,1)} fusion(bf16[8,2,128,640]{3,2,1,0:T(8,128)(2,1)} %bitcast.33, pred[8,2]{1,0:T(8,128)(4,1)S(1)} %copy.7), kind=kLoop, calls=%fused_computation.5 | loop fusion | flops 1310720 | bytes 5242896 | tf_op jit(solution)/shard_map/jit(_take)/select_n | solution.py:56
  17.8 5.2 %all-to-all-start = ((bf16[8,2,128,640]{3,2,1,0:T(8,128)(2,1)}), bf16[8,2,128,640]{3,2,1,0:T(8,128)(2,1)}, u32[]{:S(2)}, u32[]{:S(2)}) async-start(bf16[8,2,128,640]{3,2,1,0:T(8,128)(2,1)} %broadcast_select_fusion), calls=%async_computation | async-start | bytes 5242880 | tf_op jit(solution)/shard_map/all_to_all | solution.py:57
  23.0 0.0 reduce-scatter.2.cloned.1.call-start
  23.1 0.1 broadcast_bitcast_fusion
  23.2 32.2 %all-to-all-done = bf16[8,2,128,640]{3,2,1,0:T(8,128)(2,1)} async-done(((bf16[8,2,128,640]{3,2,1,0:T(8,128)(2,1)}), bf16[8,2,128,640]{3,2,1,0:T(8,128)(2,1)}, u32[]{:S(2)}, u32[]{:S(2)}) %all-to-all-start) | async-done | bytes 2621472 | tf_op jit(solution)/shard_map/all_to_all | solution.py:57
  55.4 2.5 gather_fusion.1
  57.9 0.3 bitcast_select_fusion
  58.2 0.0 copy-start.2
  58.2 1.0 copy-done.2
  59.3 0.0 copy-done
  59.3 3.8 %convolution_bitcast_fusion = f32[1024,1024]{0,1:T(8,128)} fusion(bf16[1024,640]{1,0:T(8,128)(2,1)S(1)} %bitcast_select_fusion, bf16[1024,640]{1,0:T(8,128)(2,1)S(1)} %copy-done), kind=kOutput, calls=%fused_computation.6 | convolution fusion | flops 1342177280 | bytes 6815744 | tf_op jit(solution)/shard_map/dot_general | solution.py:67
  63.1 0.0 copy-start.4
  63.1 0.0 reduce-scatter.2.cloned.1.call-update
  63.2 0.0 all-gather.2.cloned.1.call-start
  63.2 0.7 fusion.7
  63.9 0.0 copy-done.4
  63.9 0.1 and_select_fusion.1
  64.0 0.1 select_reduce_fusion.1
  64.1 0.1 fusion.4
  64.2 75.9 %reduce-scatter.2.cloned.1.call-done = f32[256,1024]{0,1:T(8,128)} async-done(((f32[1024,1024]{0,1:T(8,128)}), f32[256,1024]{0,1:T(8,128)}) %reduce-scatter.2.cloned.1.call-update) | async-done | bytes 1048592 | tf_op jit(solution)/shard_map/reduce_scatter | solution.py:66
  140.1 0.0 copy-start.1
  140.1 1.5 multiply_reduce_fusion
  141.6 1.5 fusion
  143.1 0.0 copy-done.1
  143.1 1.1 subtract_convert_fusion
  144.3 0.0 all-gather.2.cloned.1.call-update
  144.3 46.9 %all-gather.2.cloned.1.call-done = bf16[1024,1024]{0,1:T(8,128)(2,1)} async-done(((bf16[256,1024]{0,1:T(8,128)(2,1)}), bf16[1024,1024]{0,1:T(8,128)(2,1)}) %all-gather.2.cloned.1.call-update) | async-done | bytes 2097168 | tf_op jit(solution)/shard_map/all_gather | solution.py:78
  191.2 3.4 %convolution_convert_fusion = bf16[1024,640]{1,0:T(8,128)(2,1)S(1)} fusion(bf16[1024,1024]{0,1:T(8,128)(2,1)} %all-gather.2.cloned.1.call-done, bf16[1024,640]{1,0:T(8,128)(2,1)S(1)} %copy-done), kind=kOutput, calls=%fused_computation.7 | convolution fusion | flops 1342832640 | bytes 4718592 | tf_op jit(solution)/shard_map/dot_general | solution.py:81
  194.6 1.8 broadcast_in_dim.55
  196.4 3.1 scatter_fusion
  199.4 0.0 copy-start.3
  199.4 4.5 %all-to-all-start.1 = ((bf16[8,2,128,640]{3,2,1,0:T(8,128)(2,1)}), bf16[8,2,128,640]{3,2,1,0:T(8,128)(2,1)}, u32[]{:S(2)}, u32[]{:S(2)}) async-start(bf16[8,2,128,640]{3,2,1,0:T(8,128)(2,1)} %bitcast.32), calls=%async_computation.2 | async-start | bytes 5242880 | tf_op jit(solution)/shard_map/all_to_all | solution.py:89
  203.9 0.6 subtract_reduce_fusion
  204.5 62.9 %psum.7 = f32[]{:T(128)} all-reduce(f32[]{:T(128)} %subtract_reduce_fusion), channel_id=1, replica_groups=mesh['dp'=4,'proto'=8] {'dp','proto'}, use_global_device_ids=true, to_apply=%region_8.9 | all-reduce | flops 1 | bytes 8 | tf_op jit(solution)/shard_map/psum | solution.py:79
  268.1 0.0 copy-done.3
  268.1 4.5 %convolution_convert_fusion.1 = bf16[1024,640]{1,0:T(8,128)(2,1)} fusion(bf16[1024,1024]{0,1:T(8,128)(2,1)} %all-gather.2.cloned.1.call-done, bf16[1024,640]{1,0:T(8,128)(2,1)S(1)} %copy-done.3), kind=kOutput, calls=%fused_computation.8 | convolution fusion | flops 1342832640 | bytes 4718592 | tf_op jit(solution)/shard_map/dot_general | solution.py:80
  272.6 0.0 all-to-all-done.1
  272.6 4.6 %bitcast_convert_fusion = f32[16,128,640]{2,1,0:T(8,128)} fusion(bf16[8,2,128,640]{3,2,1,0:T(8,128)(2,1)} %all-to-all-done.1), kind=kLoop, calls=%fused_computation.4 | loop fusion | flops 1310720 | bytes 7864320 | tf_op jit(solution)/shard_map/convert_element_type | solution.py:99
  277.3 5.2 %broadcast_in_dim.54 = f32[32,128,640]{2,1,0:T(8,128)} broadcast(f32[]{:T(128)} %constant.115.clone.1), dimensions={} | broadcast | bytes 10485764 | tf_op jit(solution)/shard_map/broadcast_in_dim | solution.py:97
  282.5 10.5 %scatter_fusion.1 = f32[32,128,640]{2,1,0:T(8,128)} fusion(f32[32,128,640]{2,1,0:T(8,128)} %broadcast_in_dim.54, s32[16]{0:T(128)S(1)} %fusion.8, f32[16,128,640]{2,1,0:T(8,128)} %bitcast_convert_fusion), kind=kCustom, calls=%fused_computation.3 | custom fusion | flops 1310720 | bytes 15728704 | tf_op jit(solution)/shard_map/scatter-add | solution.py:99
  292.9 7.1 %convert_element_type.36 = bf16[32,128,640]{2,1,0:T(8,128)(2,1)} convert(f32[32,128,640]{2,1,0:T(8,128)} %scatter_fusion.1) | non-fusion elementwise | flops 2621440 | bytes 15728640 | tf_op jit(solution)/shard_map/convert_element_type | solution.py:101
  (7 shorter events, 0.1 us)
Async XLA Ops:
  7.2 52.1 %copy-start = (bf16[1024,640]{1,0:T(8,128)(2,1)S(1)}, bf16[1024,640]{1,0:T(8,128)(2,1)}, u32[]{:S(2)}) copy-start(bf16[1024,640]{1,0:T(8,128)(2,1)} %param.4) | copy-start | bytes 3932164
  17.8 37.5 %all-to-all-start = ((bf16[8,2,128,640]{3,2,1,0:T(8,128)(2,1)}), bf16[8,2,128,640]{3,2,1,0:T(8,128)(2,1)}, u32[]{:S(2)}, u32[]{:S(2)}) async-start(bf16[8,2,128,640]{3,2,1,0:T(8,128)(2,1)} %broadcast_select_fusion), calls=%async_computation | async-start | bytes 5242880 | tf_op jit(solution)/shard_map/all_to_all | solution.py:57
  23.0 117.1 %reduce-scatter.2.cloned.1.call-start = ((), (), s32[]{:S(2)}) async-start(), calls=%async_computation.3 | async-start | bytes 5242880 | tf_op jit(solution)/shard_map/reduce_scatter | solution.py:66
  58.2 1.1 copy-start.2
  63.1 0.8 copy-start.4
  63.2 128.0 %all-gather.2.cloned.1.call-start = ((), (), s32[]{:S(2)}) async-start(), calls=%async_computation.4 | async-start | bytes 2621440 | tf_op jit(solution)/shard_map/all_gather | solution.py:78
  140.1 3.0 copy-start.1
  199.4 68.7 %copy-start.3 = (bf16[1024,640]{1,0:T(8,128)(2,1)S(1)}, bf16[1024,640]{1,0:T(8,128)(2,1)}, u32[]{:S(2)}) copy-start(bf16[1024,640]{1,0:T(8,128)(2,1)} %copy-done.2) | copy-start | bytes 3932164
  199.4 73.2 %all-to-all-start.1 = ((bf16[8,2,128,640]{3,2,1,0:T(8,128)(2,1)}), bf16[8,2,128,640]{3,2,1,0:T(8,128)(2,1)}, u32[]{:S(2)}, u32[]{:S(2)}) async-start(bf16[8,2,128,640]{3,2,1,0:T(8,128)(2,1)} %bitcast.32), calls=%async_computation.2 | async-start | bytes 5242880 | tf_op jit(solution)/shard_map/all_to_all | solution.py:89
Sparse Core Ops, SparseCore 0:
  63.3 76.7 reduce-scatter.1
  144.4 46.7 all-gather.1
where the time goes:
time: 309 us; the launch traced here: 308 us
  waiting for transfers between devices  155 us (50%)
  blocking collectives  62.9 us (20%)
  other arithmetic  33.1 us (11%)
  local copies, waits for them, and re-layouts  19.5 us (6%)
  between operations  15.9 us (5%)
  matrix products  11.7 us (4%)
  starting transfers between devices  9.76 us (3%)
    reduce_scatter x1, waiting for transfers between devices, body(): lax.psum_scatter(lax.dot_general(embeddings, tiles, (((1,), (1,)), ((), (...  75.9 us
    psum x1, blocking collectives, body(): loss = lax.psum(loss_part, ('dp', 'proto')) / total_rows  62.9 us
    all_gather x1, waiting for transfers between devices, body(): dz_block = lax.all_gather(dz_rows, 'dp', axis=0, tiled=True)  46.9 us
    all_to_all x1, waiting for transfers between devices, body(): lax.all_to_all(outgoing, 'proto', split_axis=0, concat_axis=0, tiled=True)  32.2 us
    scatter-add x1, other arithmetic, body(): accum = jnp.zeros((tiles_here, TILE, width), jnp.float32).at[select.resha...  10.5 us
    convert_element_type x1, other arithmetic, body(): grad_table = accum.reshape(tiles_here * TILE, width).astype(jnp.bfloat16)  7.1 us
  transfers between devices with their start and end apart: 4, of which 3 were waited for; matrix products, arithmetic and copies ran while one was open for 2% of the time, Pallas kernels for 0%

commit v1 on v0

--- a/solution.py
+++ b/solution.py
@@ -54,7 +54,19 @@
     select = jnp.sum(match.astype(jnp.int32) * local[:, :, None], axis=1)
     shaped_table = table.reshape(tiles_here, TILE, width)
     outgoing = jnp.take(shaped_table, select.reshape(-1), axis=0).reshape(groups, CAP, TILE, width)
-    incoming = lax.all_to_all(outgoing, "proto", split_axis=0, concat_axis=0, tiled=True)
+    ways, here = (lax.axis_size("proto"), lax.axis_index("proto"))
+    width_2 = outgoing.shape[0] // ways
+    dims = list(outgoing.shape)
+    dims[0] = width_2
+    height = dims[0]
+    dims[0] = height * ways
+    full = jnp.zeros(dims, outgoing.dtype)
+    for mask in range(ways):
+        part_2 = lax.dynamic_slice_in_dim(outgoing, (here ^ mask) * width_2, width_2, axis=0)
+        if mask:
+            part_2 = lax.ppermute(part_2, "proto", [(d, d ^ mask) for d in range(ways)])
+        full = lax.dynamic_update_slice_in_dim(full, part_2, (here ^ mask) * height, axis=0)
+    incoming = full
     my_ids = lax.dynamic_index_in_dim(tile_lists, me, 0, keepdims=False)
     my_owner = lax.dynamic_index_in_dim(owners, me, 0, keepdims=False)
     my_rank = lax.dynamic_index_in_dim(rank, me, 0, keepdims=False)

time: 309 us -> 318 us (1.029)
  local copies, waits for them, and re-layouts: 19.5 us -> 27.6 us
    ppermute x0 -> x7, waiting for transfers between devices: none -> 32.6 us  [body(): part_2 = lax.ppermute(part_2, 'proto', [(d, d ^ mask) for d in range(ways)])]
    all_to_all x1 -> x0, waiting for transfers between devices: 32.2 us -> none  [body(): lax.all_to_all(outgoing, 'proto', split_axis=0, concat_axis=0, tiled=True)]
    ppermute x0 -> x7, starting transfers between devices: none -> 7.55 us  [body(): part_2 = lax.ppermute(part_2, 'proto', [(d, d ^ mask) for d in range(ways)])]
    dynamic_update_slice x0 -> x7, local copies, waits for them, and re-layouts: none -> 5.27 us  [body(): lax.dynamic_update_slice_in_dim(full, part_2, (here ^ mask) * height, axi...]
    all_to_all x1 -> x0, starting transfers between devices: 5.17 us -> none  [body(): lax.all_to_all(outgoing, 'proto', split_axis=0, concat_axis=0, tiled=True)]
  transfers between devices with their start and end apart: 4 -> 10, of which waited for: 3 -> 5; matrix products, arithmetic and copies ran while one was open for 2% -> 3% of each run, Pallas kernels for 0% -> 0%
where the time goes in v1:
time: 318 us
  waiting for transfers between devices  156 us (49%)
  blocking collectives  62.9 us (20%)
  other arithmetic  31.6 us (10%)
  local copies, waits for them, and re-layouts  27.6 us (9%)
  between operations  16 us (5%)
  starting transfers between devices  12.1 us (4%)
  matrix products  11.7 us (4%)
    reduce_scatter x1, waiting for transfers between devices, body(): lax.psum_scatter(lax.dot_general(embeddings, tiles, (((1,), (1,)), ((), (...  76.3 us
    psum x1, blocking collectives, body(): loss = lax.psum(loss_part, ('dp', 'proto')) / total_rows  62.9 us
    all_gather x1, waiting for transfers between devices, body(): dz_block = lax.all_gather(dz_rows, 'dp', axis=0, tiled=True)  46.9 us
    ppermute x7, waiting for transfers between devices, body(): part_2 = lax.ppermute(part_2, 'proto', [(d, d ^ mask) for d in range(ways)])  32.6 us
    scatter-add x1, other arithmetic, body(): accum = jnp.zeros((tiles_here, TILE, width), jnp.float32).at[select.resha...  10.5 us
    ppermute x7, starting transfers between devices, body(): part_2 = lax.ppermute(part_2, 'proto', [(d, d ^ mask) for d in range(ways)])  7.55 us
    convert_element_type x1, other arithmetic, body(): grad_table = accum.reshape(tiles_here * TILE, width).astype(jnp.bfloat16)  7.1 us
  transfers between devices with their start and end apart: 10, of which 5 were waited for; matrix products, arithmetic and copies ran while one was open for 3% of the time, Pallas kernels for 0%

profile of v1, /device:TPU:0, one launch (start us, length us, event | category | flops | bytes accessed | tf_op | source)
XLA Modules:
  0.0 317.7 jit_solution(11610583997041148877)
XLA Ops:
  7.2 0.0 copy-start
  7.2 0.0 reduce-scatter.2.cloned.1.call-start
  7.3 0.8 add_select_fusion
  8.0 0.7 broadcast_compare_fusion
  8.7 0.3 convert_reduce_fusion
  9.0 0.2 select_reduce_fusion.2
  9.2 0.1 copy.8
  9.3 0.1 copy.7
  9.4 0.1 reshape.136
  9.5 4.8 %gather_fusion = bf16[16,128,640]{2,1,0:T(8,128)(2,1)} fusion(bf16[32,128,640]{2,1,0:T(8,128)(2,1)} %bitcast.36, s32[1024]{0:T(1024)S(1)} %pad_clamp_fusion.1), kind=kCustom, calls=%fused_computation | custom fusion | bytes 5242944 | tf_op jit(solution)/shard_map/jit(_take)/gather | solution.py:56
  14.4 2.1 broadcast_select_fusion
  16.4 1.8 broadcast_in_dim.54
  18.2 1.0 constant_dynamic-slice_fusion.1
  19.2 3.3 %collective-permute-start.6 = (bf16[1,2,128,640]{3,2,1,0:T(8,128)(2,1)S(1)}, bf16[1,2,128,640]{3,2,1,0:T(8,128)(2,1)S(1)}, u32[]{:S(2)}, u32[]{:S(2)}) collective-permute-start(bf16[1,2,128,640]{3,2,1,0:T(8,128)(2,1)S(1)} %get-tuple-element.9), channel_id=1, source_target_pairs={{0,7},{1,6},{2,5},{3,4},{4,3},{5,2},{6,1},{7,0},{8,15},{9,14},{10,... | collective-permute-start | bytes 983048 | tf_op jit(solution)/shard_map/ppermute | solution.py:67
  22.6 0.6 collective-permute-start.5
  23.1 1.4 collective-permute-start.2
  24.6 0.3 collective-permute-start.1
  24.9 0.2 collective-permute-start
  25.0 0.1 broadcast_bitcast_fusion
  25.1 1.4 collective-permute-done
  26.5 1.7 collective-permute-start.3
  28.2 0.8 constant_dynamic-update-slice_fusion.6
  29.0 23.7 %collective-permute-done.1 = bf16[1,2,128,640]{3,2,1,0:T(8,128)(2,1)S(1)} collective-permute-done((bf16[1,2,128,640]{3,2,1,0:T(8,128)(2,1)S(1)}, bf16[1,2,128,640]{3,2,1,0:T(8,128)(2,1)S(1)}, u32[]{:S(2)}, u32[]{:S(2)}) %collective-permute-start.1) | collective-permute-done | bytes 327712 | tf_op jit(solution)/shard_map/ppermute | solution.py:67
  52.7 0.0 collective-permute-start.4
  52.7 0.8 constant_dynamic-update-slice_fusion.5
  53.5 0.0 collective-permute-done.2
  53.5 0.8 constant_dynamic-update-slice_fusion.4
  54.3 0.0 collective-permute-done.3
  54.3 0.8 constant_dynamic-update-slice_fusion.3
  55.0 7.5 %collective-permute-done.4 = bf16[1,2,128,640]{3,2,1,0:T(8,128)(2,1)S(1)} collective-permute-done((bf16[1,2,128,640]{3,2,1,0:T(8,128)(2,1)S(1)}, bf16[1,2,128,640]{3,2,1,0:T(8,128)(2,1)S(1)}, u32[]{:S(2)}, u32[]{:S(2)}) %collective-permute-start.4) | collective-permute-done | bytes 327712 | tf_op jit(solution)/shard_map/ppermute | solution.py:67
  62.5 0.8 constant_dynamic-update-slice_fusion.2
  63.2 0.0 collective-permute-done.5
  63.2 0.8 constant_dynamic-update-slice_fusion.1
  64.0 0.0 collective-permute-done.6
  64.0 0.8 constant_dynamic-update-slice_fusion
  64.7 2.5 gather_fusion.1
  67.3 0.3 bitcast_select_fusion
  67.6 0.0 copy-start.2
  67.6 1.0 copy-done.2
  68.7 3.8 %convolution_bitcast_fusion = f32[1024,1024]{0,1:T(8,128)} fusion(bf16[1024,640]{1,0:T(8,128)(2,1)S(1)} %bitcast_select_fusion, bf16[1024,640]{1,0:T(8,128)(2,1)S(1)} %copy-done), kind=kOutput, calls=%fused_computation.6 | convolution fusion | flops 1342177280 | bytes 6815744 | tf_op jit(solution)/shard_map/dot_general | solution.py:79
  72.5 0.0 reduce-scatter.2.cloned.1.call-update
  72.5 0.0 all-gather.2.cloned.1.call-start
  72.6 0.7 fusion.9
  73.3 0.1 and_select_fusion.1
  73.4 0.1 select_reduce_fusion.1
  73.5 0.1 fusion.4
  73.5 76.3 %reduce-scatter.2.cloned.1.call-done = f32[256,1024]{0,1:T(8,128)} async-done(((f32[1024,1024]{0,1:T(8,128)}), f32[256,1024]{0,1:T(8,128)}) %reduce-scatter.2.cloned.1.call-update) | async-done | bytes 1048592 | tf_op jit(solution)/shard_map/reduce_scatter | solution.py:78
  149.8 1.5 multiply_reduce_fusion
  151.3 1.5 fusion
  152.8 1.1 subtract_convert_fusion
  154.0 0.0 all-gather.2.cloned.1.call-update
  154.0 46.9 %all-gather.2.cloned.1.call-done = bf16[1024,1024]{0,1:T(8,128)(2,1)} async-done(((bf16[256,1024]{0,1:T(8,128)(2,1)}), bf16[1024,1024]{0,1:T(8,128)(2,1)}) %all-gather.2.cloned.1.call-update) | async-done | bytes 2097168 | tf_op jit(solution)/shard_map/all_gather | solution.py:90
  200.9 3.4 %convolution_convert_fusion = bf16[1024,640]{1,0:T(8,128)(2,1)S(1)} fusion(bf16[1024,1024]{0,1:T(8,128)(2,1)} %all-gather.2.cloned.1.call-done, bf16[1024,640]{1,0:T(8,128)(2,1)S(1)} %copy-done), kind=kOutput, calls=%fused_computation.7 | convolution fusion | flops 1342832640 | bytes 4718592 | tf_op jit(solution)/shard_map/dot_general | solution.py:93
  204.3 1.8 broadcast_in_dim.59
  206.1 3.1 scatter_fusion
  209.1 4.5 %all-to-all-start = ((bf16[8,2,128,640]{3,2,1,0:T(8,128)(2,1)}), bf16[8,2,128,640]{3,2,1,0:T(8,128)(2,1)}, u32[]{:S(2)}, u32[]{:S(2)}) async-start(bf16[8,2,128,640]{3,2,1,0:T(8,128)(2,1)} %bitcast.32), calls=%async_computation.1 | async-start | bytes 5242880 | tf_op jit(solution)/shard_map/all_to_all | solution.py:101
  213.6 0.6 subtract_reduce_fusion
  214.3 62.9 %psum.7 = f32[]{:T(128)} all-reduce(f32[]{:T(128)} %subtract_reduce_fusion), channel_id=1, replica_groups=mesh['dp'=4,'proto'=8] {'dp','proto'}, use_global_device_ids=true, to_apply=%region_8.9 | all-reduce | flops 1 | bytes 8 | tf_op jit(solution)/shard_map/psum | solution.py:91
  277.8 4.5 %convolution_convert_fusion.1 = bf16[1024,640]{1,0:T(8,128)(2,1)} fusion(bf16[1024,1024]{0,1:T(8,128)(2,1)} %all-gather.2.cloned.1.call-done, bf16[1024,640]{1,0:T(8,128)(2,1)S(1)} %copy-done.3), kind=kOutput, calls=%fused_computation.8 | convolution fusion | flops 1342832640 | bytes 4718592 | tf_op jit(solution)/shard_map/dot_general | solution.py:92
  282.3 0.0 all-to-all-done
  282.3 4.6 %bitcast_convert_fusion = f32[16,128,640]{2,1,0:T(8,128)} fusion(bf16[8,2,128,640]{3,2,1,0:T(8,128)(2,1)} %all-to-all-done), kind=kLoop, calls=%fused_computation.4 | loop fusion | flops 1310720 | bytes 7864320 | tf_op jit(solution)/shard_map/convert_element_type | solution.py:111
  287.0 5.2 %broadcast_in_dim.58 = f32[32,128,640]{2,1,0:T(8,128)} broadcast(f32[]{:T(128)} %constant.129.clone.1), dimensions={} | broadcast | bytes 10485764 | tf_op jit(solution)/shard_map/broadcast_in_dim | solution.py:109
  292.2 10.5 %scatter_fusion.1 = f32[32,128,640]{2,1,0:T(8,128)} fusion(f32[32,128,640]{2,1,0:T(8,128)} %broadcast_in_dim.58, s32[16]{0:T(128)S(1)} %fusion.5, f32[16,128,640]{2,1,0:T(8,128)} %bitcast_convert_fusion), kind=kCustom, calls=%fused_computation.3 | custom fusion | flops 1310720 | bytes 15728704 | tf_op jit(solution)/shard_map/scatter-add | solution.py:111
  302.6 7.1 %convert_element_type.36 = bf16[32,128,640]{2,1,0:T(8,128)(2,1)} convert(f32[32,128,640]{2,1,0:T(8,128)} %scatter_fusion.1) | non-fusion elementwise | flops 2621440 | bytes 15728640 | tf_op jit(solution)/shard_map/convert_element_type | solution.py:113
  (14 shorter events, 0.1 us)
Async XLA Ops:
  7.2 61.5 %copy-start = (bf16[1024,640]{1,0:T(8,128)(2,1)S(1)}, bf16[1024,640]{1,0:T(8,128)(2,1)}, u32[]{:S(2)}) copy-start(bf16[1024,640]{1,0:T(8,128)(2,1)} %param.4) | copy-start | bytes 3932164
  7.2 142.6 %reduce-scatter.2.cloned.1.call-start = ((), (), s32[]{:S(2)}) async-start(), calls=%async_computation.2 | async-start | bytes 5242880 | tf_op jit(solution)/shard_map/reduce_scatter | solution.py:78
  19.2 44.8 %collective-permute-start.6 = (bf16[1,2,128,640]{3,2,1,0:T(8,128)(2,1)S(1)}, bf16[1,2,128,640]{3,2,1,0:T(8,128)(2,1)S(1)}, u32[]{:S(2)}, u32[]{:S(2)}) collective-permute-start(bf16[1,2,128,640]{3,2,1,0:T(8,128)(2,1)S(1)} %get-tuple-element.9), channel_id=1, source_target_pairs={{0,7},{1,6},{2,5},{3,4},{4,3},{5,2},{6,1},{7,0},{8,15},{9,14},{10,... | collective-permute-start | bytes 983048 | tf_op jit(solution)/shard_map/ppermute | solution.py:67
  22.6 40.7 %collective-permute-start.5 = (bf16[1,2,128,640]{3,2,1,0:T(8,128)(2,1)S(1)}, bf16[1,2,128,640]{3,2,1,0:T(8,128)(2,1)S(1)}, u32[]{:S(2)}, u32[]{:S(2)}) collective-permute-start(bf16[1,2,128,640]{3,2,1,0:T(8,128)(2,1)S(1)} %get-tuple-element.10), channel_id=1, source_target_pairs={{0,6},{1,7},{2,4},{3,5},{4,2},{5,3},{6,0},{7,1},{8,14},{9,15},{10,... | collective-permute-start | bytes 983048 | tf_op jit(solution)/shard_map/ppermute | solution.py:67
  23.1 30.4 %collective-permute-start.2 = (bf16[1,2,128,640]{3,2,1,0:T(8,128)(2,1)S(1)}, bf16[1,2,128,640]{3,2,1,0:T(8,128)(2,1)S(1)}, u32[]{:S(2)}, u32[]{:S(2)}) collective-permute-start(bf16[1,2,128,640]{3,2,1,0:T(8,128)(2,1)S(1)} %get-tuple-element.13), channel_id=1, source_target_pairs={{0,3},{1,2},{2,1},{3,0},{4,7},{5,6},{6,5},{7,4},{8,11},{9,10},{10,... | collective-permute-start | bytes 983048 | tf_op jit(solution)/shard_map/ppermute | solution.py:67
  24.6 28.2 %collective-permute-start.1 = (bf16[1,2,128,640]{3,2,1,0:T(8,128)(2,1)S(1)}, bf16[1,2,128,640]{3,2,1,0:T(8,128)(2,1)S(1)}, u32[]{:S(2)}, u32[]{:S(2)}) collective-permute-start(bf16[1,2,128,640]{3,2,1,0:T(8,128)(2,1)S(1)} %get-tuple-element.14), channel_id=1, source_target_pairs={{0,2},{1,3},{2,0},{3,1},{4,6},{5,7},{6,4},{7,5},{8,10},{9,11},{10,... | collective-permute-start | bytes 983048 | tf_op jit(solution)/shard_map/ppermute | solution.py:67
  24.9 1.6 collective-permute-start
  26.5 27.8 %collective-permute-start.3 = (bf16[1,2,128,640]{3,2,1,0:T(8,128)(2,1)S(1)}, bf16[1,2,128,640]{3,2,1,0:T(8,128)(2,1)S(1)}, u32[]{:S(2)}, u32[]{:S(2)}) collective-permute-start(bf16[1,2,128,640]{3,2,1,0:T(8,128)(2,1)S(1)} %get-tuple-element.12), channel_id=1, source_target_pairs={{0,4},{1,5},{2,6},{3,7},{4,0},{5,1},{6,2},{7,3},{8,12},{9,13},{10,... | collective-permute-start | bytes 983048 | tf_op jit(solution)/shard_map/ppermute | solution.py:67
  52.7 9.7 %collective-permute-start.4 = (bf16[1,2,128,640]{3,2,1,0:T(8,128)(2,1)S(1)}, bf16[1,2,128,640]{3,2,1,0:T(8,128)(2,1)S(1)}, u32[]{:S(2)}, u32[]{:S(2)}) collective-permute-start(bf16[1,2,128,640]{3,2,1,0:T(8,128)(2,1)S(1)} %get-tuple-element.11), channel_id=1, source_target_pairs={{0,5},{1,4},{2,7},{3,6},{4,1},{5,0},{6,3},{7,2},{8,13},{9,12},{10,... | collective-permute-start | bytes 983048 | tf_op jit(solution)/shard_map/ppermute | solution.py:67
  67.6 1.1 copy-start.2
  72.5 0.8 copy-start.4
  72.5 128.4 %all-gather.2.cloned.1.call-start = ((), (), s32[]{:S(2)}) async-start(), calls=%async_computation.3 | async-start | bytes 2621440 | tf_op jit(solution)/shard_map/all_gather | solution.py:90
  149.8 3.0 copy-start.1
  209.1 68.7 %copy-start.3 = (bf16[1024,640]{1,0:T(8,128)(2,1)S(1)}, bf16[1024,640]{1,0:T(8,128)(2,1)}, u32[]{:S(2)}) copy-start(bf16[1024,640]{1,0:T(8,128)(2,1)} %copy-done.2) | copy-start | bytes 3932164
  209.1 73.2 %all-to-all-start = ((bf16[8,2,128,640]{3,2,1,0:T(8,128)(2,1)}), bf16[8,2,128,640]{3,2,1,0:T(8,128)(2,1)}, u32[]{:S(2)}, u32[]{:S(2)}) async-start(bf16[8,2,128,640]{3,2,1,0:T(8,128)(2,1)} %bitcast.32), calls=%async_computation.1 | async-start | bytes 5242880 | tf_op jit(solution)/shard_map/all_to_all | solution.py:101
Sparse Core Ops, SparseCore 0:
  72.6 77.1 reduce-scatter.1
  154.1 46.7 all-gather.1
